TPU v7x, 128 devices: a whole 4x4x4 slice. The times are simulated.
128 devices in a mesh: gen: 8 (over y, core), voc: 16 (over x, z).
Axes of the slice: x: 4, y: 4, z: 4, core: 2. Of those that a mesh axis runs over, the one named last changes fastest.
Arguments:
- features: bfloat16 [8192, 24, 128], P(('gen', 'voc')), may hold values from -6 to 6
- target: int32 [8192], P(('gen', 'voc')), may hold values from -1 to 511, as said below
- extents: int32 [8192, 3], P(('gen', 'voc')), may hold values from 0 to 24, as said below
- w_pre: bfloat16 [896, 1536], replicated, may hold values from -0.1875 to 0.1875
- biases: float32 [1536], replicated, may hold values from -1.5 to 1.5
- snake_params: float32 [2, 1536], replicated, may hold values from 0.4 to 2.5
- w_up: bfloat16 [1536, 6144], replicated, may hold values from -0.109375 to 0.109375
- up_bias: float32 [768], replicated, may hold values from -1.5 to 1.5
Outputs:
- waves: bfloat16 [8192, 96, 768], P(('gen', 'voc'))
Inputs may be any that keep to these rules, and one draw needn't show every extreme that they name: Within each gen group every (voc index, slot) pair target[i] = voc index * 32 + slot is named by exactly one generator slot; -1 marks an empty generator slot. No generator device names one vocoder device more than 4 times, and in every group some device does so exactly 4 times for each vocoder device. `extents`: column 0 is 24 except for the last segment of an utterance; columns 1 and 2 are 0 where the stream neighbour belongs to another utterance and equal its column 0 otherwise; all zero for empty slots.
All inputs are finite; a program needn't handle non-finite values.
Results may differ from a plain program's by a relative error of at most 0.0048.
Values may be sent and summed in bfloat16 or wider, within the bound.
No kernel may reach another device: no remote copies, remote signals or barrier semaphores. Data moves between devices by JAX's collectives and lax.ppermute only.
A program may use at most 192 MiB of HBM per device.

v0:
```python
import jax
import jax.numpy as jnp
from jax import lax
from jax.sharding import PartitionSpec as P

UP = 4
KPRE = 7
RIM = 4


def passed_along(value, axis, by):
    count = lax.axis_size(axis)
    return lax.ppermute(value, axis, [(i, (i + by) % count) for i in range(count)])


def stacked_taps(values, kernel):
    length = values.shape[1] - (kernel - 1)
    pieces = [values[:, tap_index : tap_index + length] for tap_index in range(kernel)]
    return jnp.concatenate(pieces, axis=2)


def convolve(values, weight, kernel):
    stacked = stacked_taps(values, kernel)
    flattened = stacked.reshape(-1, stacked.shape[2])
    result = jnp.dot(flattened, weight, preferred_element_type=jnp.float32)
    return result.reshape(stacked.shape[0], stacked.shape[1], weight.shape[1])


def snake_act(values, alpha, beta):
    return values + jnp.square(jnp.sin(alpha * values)) / beta


def window_mask(extent_rows, seg_len):
    rim_cells = jnp.arange(RIM, dtype=jnp.int32)
    cells = jnp.arange(seg_len, dtype=jnp.int32)
    before = rim_cells[None, :] + seg_len - RIM < extent_rows[:, 1:2]
    own_part = cells[None, :] < extent_rows[:, 0:1]
    after = rim_cells[None, :] < extent_rows[:, 2:3]
    return jnp.concatenate([before, own_part, after], axis=1).astype(jnp.float32)


def trunk(window, frame_mask, w_pre, biases, snake_params):
    first = (KPRE - 1) // 2
    span = window.shape[1]
    inputs = window * frame_mask[:, :, None].astype(jnp.bfloat16)
    hidden = frame_mask[:, first : span - first, None] * (convolve(inputs, w_pre, KPRE) + biases)
    return snake_act(hidden, snake_params[0], snake_params[1]).astype(jnp.bfloat16)


def upsample(activations, seg_mask, w_up, up_bias):
    projected = jnp.dot(
        activations.reshape(-1, activations.shape[2]), w_up, preferred_element_type=jnp.float32
    )
    projected = projected.reshape(
        activations.shape[0], activations.shape[1], 2 * UP, up_bias.shape[0]
    )
    centre = projected[:, 1:-1, UP // 2 : UP // 2 + UP]
    side = jnp.concatenate([projected[:, :-2, 3 * UP // 2 :], projected[:, 2:, : UP // 2]], axis=2)
    samples = seg_mask[:, :, None, None] * (centre + side + up_bias)
    return samples.astype(jnp.bfloat16).reshape(activations.shape[0], -1, up_bias.shape[0])


def move_rows(selection, values):
    moved = jnp.dot(
        selection.astype(jnp.bfloat16),
        values.reshape(values.shape[0], -1),
        preferred_element_type=jnp.float32,
    )
    return moved.astype(jnp.bfloat16)


def on_device(features, target, extents, w_pre, biases, snake_params, w_up, up_bias):
    src_cap, seg_len, feat_width = features.shape
    slots = src_cap // 2
    workers = lax.axis_size("voc")
    capacity = src_cap // workers
    used = target >= 0
    worker_of = jnp.where(used, target // slots, -1)
    worker_hot = (worker_of[:, None] == jnp.arange(workers, dtype=jnp.int32)[None, :]).astype(
        jnp.int32
    )
    earlier = jnp.cumsum(worker_hot, axis=0) - worker_hot
    send_row = jnp.where(used, worker_of * capacity + jnp.sum(earlier * worker_hot, axis=1), -1)
    selector = send_row[None, :] == jnp.arange(src_cap, dtype=jnp.int32)[:, None]
    details = jnp.concatenate([jnp.where(used, target % slots + 1, 0)[:, None], extents], axis=1)
    send_feat = move_rows(selector, features).reshape(workers, capacity, seg_len, feat_width)
    send_info = jnp.dot(selector.astype(jnp.int32), details).reshape(workers, capacity, 4)
    got_feat, got_info = (
        lax.all_to_all(send_feat, "voc", split_axis=0, concat_axis=0, tiled=True),
        lax.all_to_all(send_info, "voc", split_axis=0, concat_axis=0, tiled=True),
    )
    got_info = got_info.reshape(src_cap, 4)
    placing = got_info[:, 0][None, :] - 1 == jnp.arange(slots, dtype=jnp.int32)[:, None]
    seg_feat = move_rows(placing, got_feat.reshape(src_cap, -1)).reshape(slots, seg_len, feat_width)
    seg_ext = jnp.dot(placing.astype(jnp.int32), got_info)[:, 1:]
    position = lax.axis_index(("gen", "voc"))
    count_all = lax.axis_size(("gen", "voc"))
    prev_tail = passed_along(seg_feat[:, seg_len - RIM :], ("gen", "voc"), 1)
    prev_tail = jnp.where(position == 0, jnp.roll(prev_tail, 1, axis=0), prev_tail)
    next_head = passed_along(seg_feat[:, :RIM], ("gen", "voc"), -1)
    next_head = jnp.where(position == count_all - 1, jnp.roll(next_head, -1, axis=0), next_head)
    frame_mask = window_mask(seg_ext, seg_len)
    window = jnp.concatenate([prev_tail, seg_feat, next_head], axis=1)
    activations = trunk(window, frame_mask, w_pre, biases, snake_params)
    vocoded = upsample(activations, frame_mask[:, RIM : RIM + seg_len], w_up, up_bias)
    back = move_rows(placing.T, vocoded).reshape(
        workers, capacity, vocoded.shape[1], vocoded.shape[2]
    )
    home = lax.all_to_all(back, "voc", split_axis=0, concat_axis=0, tiled=True)
    waves = move_rows(selector.T, home.reshape(src_cap, -1)).reshape(
        src_cap, vocoded.shape[1], vocoded.shape[2]
    )
    return waves


def solution(mesh):
    placed = (
        P(("gen", "voc"), None, None),
        P(("gen", "voc")),
        P(("gen", "voc"), None),
        P(),
        P(),
        P(),
        P(),
        P(),
    )
    return jax.shard_map(
        on_device,
        mesh=mesh,
        in_specs=placed,
        out_specs=P(("gen", "voc"), None, None),
        check_vma=False,
    )
```

profile of v0, /device:TPU:11, one launch (start us, length us, event | category | flops | bytes accessed | tf_op | source)
XLA Modules:
  0.0 292.0 jit_solution(7866300981972765465)
XLA Ops:
  0.0 0.0 copy-start
  0.0 0.8 fusion.27
  0.8 0.1 fusion.12
  0.9 0.1 reduce_window_sum.11
  1.0 0.2 select_reduce_fusion
  1.2 0.7 fusion.26
  1.8 0.8 fusion.11
  2.7 0.1 reshape.114
  2.8 0.6 copy.18
  3.4 7.8 %all-to-all-start = ((s32[16,4,4]{1,2,0:T(4,128)}), s32[16,4,4]{1,2,0:T(4,128)S(1)}, u32[]{:S(2)}, u32[]{:S(2)}) async-start(s32[16,4,4]{1,2,0:T(4,128)} %copy.18), calls=%async_computation | async-start | bytes 65536 | tf_op jit(solution)/shard_map/all_to_all | solution.py:90
  11.2 0.8 slice_reduce_fusion.1
  12.0 1.2 fusion.5
  13.3 0.8 copy.29
  14.1 24.6 %copy.26 = bf16[6144,1536]{1,0:T(8,128)(2,1)} copy(bf16[6144,1536]{0,1:T(8,128)(2,1)} %bitcast.63) | data formatting | bytes 37748736 | tf_op jit(solution)/shard_map/dot_general | solution.py:51
  38.7 0.0 copy-start.3
  38.7 0.0 all-to-all-done
  38.7 6.8 %all-to-all-start.1 = ((bf16[16,4,24,128]{3,2,1,0:T(8,128)(2,1)}), bf16[16,4,24,128]{3,2,1,0:T(8,128)(2,1)S(1)}, u32[]{:S(2)}, u32[]{:S(2)}) async-start(bf16[16,4,24,128]{3,2,1,0:T(8,128)(2,1)} %bitcast.21), calls=%async_computation.1 | async-start | bytes 786432 | tf_op jit(solution)/shard_map/all_to_all | solution.py:89
  45.5 0.1 reshape.115
  45.6 0.1 fusion.13
  45.7 0.1 iota_compare_fusion.10
  45.8 6.2 %all-to-all-done.1 = bf16[16,4,24,128]{3,2,1,0:T(8,128)(2,1)S(1)} async-done(((bf16[16,4,24,128]{3,2,1,0:T(8,128)(2,1)}), bf16[16,4,24,128]{3,2,1,0:T(8,128)(2,1)S(1)}, u32[]{:S(2)}, u32[]{:S(2)}) %all-to-all-start.1) | async-done | bytes 393248 | tf_op jit(solution)/shard_map/all_to_all | solution.py:89
  52.0 0.2 fusion.6
  52.3 0.2 collective-permute-start
  52.5 3.4 %collective-permute-start.1 = (bf16[32,4,128]{2,0,1:T(8,128)(2,1)S(1)}, bf16[32,4,128]{2,0,1:T(8,128)(2,1)S(1)}, u32[]{:S(2)}, u32[]{:S(2)}) collective-permute-start(bf16[32,4,128]{2,0,1:T(8,128)(2,1)S(1)} %get-tuple-element.10), channel_id=1, source_target_pairs={{0,127},{1,0},{2,1},{3,2},{4,3},{5,4},{6,5},{7,6},{8,7},{9,8},{10,... | collective-permute-start | bytes 98312 | tf_op jit(solution)/shard_map/ppermute | solution.py:13
  56.0 1.0 collective-permute-done.1
  57.0 0.3 collective-permute-done
  57.3 0.2 maximum_multiply_fusion
  57.6 0.1 slice_dynamic-update-slice_fusion.5
  57.6 0.1 slice_dynamic-update-slice_fusion.4
  57.7 0.1 slice_dynamic-update-slice_fusion.3
  57.7 0.1 slice_dynamic-update-slice_fusion.2
  57.8 0.1 slice_dynamic-update-slice_fusion.1
  57.9 0.1 slice_dynamic-update-slice_fusion
  57.9 0.0 copy-done
  57.9 0.0 copy-done.3
  57.9 19.7 %fusion.3 = bf16[32,26,1536,1]{2,0,3,1:T(8,128)(2,1)S(1)} fusion(bf16[32,26,896]{2,0,1:T(8,128)(2,1)S(1)} %slice_dynamic-update-slice_fusion, bf16[896,1536]{1,0:T(8,128)(2,1)S(1)} %copy-done, f32[1536]{0:T(1024)S(1)} %get-tuple-element.6, f32[1536]{0:T(1024)S(1)} %get-tuple-element.5, f32[1536]{0:T(1024)S(1)} %copy-done.3, f32[32,26]{0,1:T(8,128)S(1)} %slice.105), kind=kOutput, calls=%fused_computation.9 | convolution fusion | flops 2299035648 | bytes 6821120 | tf_op jit(solution)/shard_map/dot_general | solution.py:25
  77.6 22.1 %fusion.31 = f32[32,26,8,768]{3,0,2,1:T(8,128)} fusion(bf16[32,26,1536,1]{2,0,3,1:T(8,128)(2,1)S(1)} %fusion.3, bf16[8,768,1536,1]{2,1,0,3:T(8,128)(2,1)} %bitcast.64), kind=kOutput, calls=%fused_computation.70 | convolution fusion | flops 15703474176 | bytes 41877504 | tf_op jit(solution)/shard_map/dot_general | solution.py:51
  99.7 0.0 copy-start.2
  99.7 4.8 %fusion.29 = (f32[32,24,2,768]{3,0,2,1:T(8,128)S(1)}, f32[32,24,2,768]{3,0,2,1:T(8,128)S(1)}) fusion(f32[32,26,8,768]{3,0,2,1:T(8,128)} %fusion.31), kind=kLoop, calls=%fused_computation.68 | loop fusion | bytes 18874368 | tf_op jit(solution)/shard_map/slice | solution.py:58
  104.6 0.0 copy-done.2
  104.6 5.7 %fusion.2 = bf16[32,24,4,768]{3,0,2,1:T(8,128)(2,1)S(1)} fusion(f32[32,26,8,768]{3,0,2,1:T(8,128)} %fusion.31, f32[32,24,2,768]{3,0,2,1:T(8,128)S(1)} %get-tuple-element.8, f32[32,24,2,768]{3,0,2,1:T(8,128)S(1)} %get-tuple-element.7, f32[768]{0:T(1024)S(1)} %copy-done.2, f32[32,24]{0,1:T(8,128)S(1)} %slice.104), kind=kLoop, calls=%fused_computation.5 | loop fusion | flops 11796480 | bytes 23599104 | tf_op jit(solution)/shard_map/convert_element_type | solution.py:60
  110.3 5.8 %copy.24 = bf16[32,24,4,768]{3,2,1,0:T(4,128)(2,1)} copy(bf16[32,24,4,768]{3,0,2,1:T(8,128)(2,1)S(1)} %fusion.2) | data formatting | bytes 9437184 | tf_op jit(solution)/shard_map/convert_element_type | solution.py:60
  116.1 6.6 %reshape_reshape.3 = bf16[32,73728]{1,0:T(8,128)(2,1)} reshape(bf16[32,24,4,768]{3,2,1,0:T(4,128)(2,1)} %copy.24) | data formatting | bytes 9437184 | tf_op jit(solution)/shard_map/reshape;reshape | solution.py:66
  122.8 8.7 %convolution_convert_fusion.1 = bf16[64,73728]{1,0:T(8,128)(2,1)} fusion(bf16[32,73728]{1,0:T(8,128)(2,1)} %reshape_reshape.3, s32[64]{0:T(128)S(1)} %add_bitcast_fusion), kind=kOutput, calls=%fused_computation.1 | convolution fusion | flops 306710528 | bytes 14156032 | tf_op jit(solution)/shard_map/dot_general | solution.py:64
  131.5 9.8 %copy.31 = bf16[8,8,96,768]{3,2,1,0:T(8,128)(2,1)} copy(bf16[8,8,96,768]{3,1,2,0:T(8,128)(2,1)} %bitcast.60) | data formatting | bytes 18874368
  141.3 117.6 %all_to_all.15 = bf16[16,4,96,768]{3,2,1,0:T(8,128)(2,1)} all-to-all(bf16[16,4,96,768]{3,2,1,0:T(8,128)(2,1)} %bitcast.61), channel_id=1, replica_groups=mesh['gen'=8,'voc'=16] {'voc'}, dimensions={0} | all-to-all | bytes 18874368 | tf_op jit(solution)/shard_map/all_to_all | solution.py:109
  258.8 13.1 %copy.32 = bf16[8,8,96,768]{3,1,2,0:T(8,128)(2,1)} copy(bf16[8,8,96,768]{3,2,1,0:T(8,128)(2,1)} %bitcast.62) | data formatting | bytes 18874368
  272.0 9.9 %convolution_convert_fusion = bf16[64,73728]{1,0:T(8,128)(2,1)} fusion(bf16[64,73728]{1,0:T(8,128)(2,1)} %bitcast.58, s32[64]{0:T(128)S(1)} %get-tuple-element.17), kind=kOutput, calls=%fused_computation | convolution fusion | flops 608702464 | bytes 18874624 | tf_op jit(solution)/shard_map/dot_general | solution.py:64
  281.9 0.0 copy-start.1
  281.9 10.0 %copy.33 = bf16[8,8,96,768]{3,2,1,0:T(8,128)(2,1)} copy(bf16[8,8,96,768]{3,1,2,0:T(8,128)(2,1)} %bitcast.59) | data formatting | bytes 18874368
  291.9 0.0 copy-done.1
  (16 shorter events, 0.2 us)
Async XLA Ops:
  0.0 57.9 %copy-start = (bf16[896,1536]{1,0:T(8,128)(2,1)S(1)}, bf16[896,1536]{1,0:T(8,128)(2,1)}, u32[]{:S(2)}) copy-start(bf16[896,1536]{1,0:T(8,128)(2,1)} %param.11) | copy-start | bytes 8257540
  3.4 35.3 %all-to-all-start = ((s32[16,4,4]{1,2,0:T(4,128)}), s32[16,4,4]{1,2,0:T(4,128)S(1)}, u32[]{:S(2)}, u32[]{:S(2)}) async-start(s32[16,4,4]{1,2,0:T(4,128)} %copy.18), calls=%async_computation | async-start | bytes 65536 | tf_op jit(solution)/shard_map/all_to_all | solution.py:90
  38.7 19.2 %copy-start.3 = (f32[1536]{0:T(1024)S(1)}, f32[1536]{0:T(1024)}, u32[]{:S(2)}) copy-start(f32[1536]{0:T(1024)} %param.12) | copy-start | bytes 18436
  38.7 13.4 %all-to-all-start.1 = ((bf16[16,4,24,128]{3,2,1,0:T(8,128)(2,1)}), bf16[16,4,24,128]{3,2,1,0:T(8,128)(2,1)S(1)}, u32[]{:S(2)}, u32[]{:S(2)}) async-start(bf16[16,4,24,128]{3,2,1,0:T(8,128)(2,1)} %bitcast.21), calls=%async_computation.1 | async-start | bytes 786432 | tf_op jit(solution)/shard_map/all_to_all | solution.py:89
  52.3 4.9 %collective-permute-start = (bf16[32,4,128]{2,0,1:T(8,128)(2,1)S(1)}, bf16[32,4,128]{2,0,1:T(8,128)(2,1)S(1)}, u32[]{:S(2)}, u32[]{:S(2)}) collective-permute-start(bf16[32,4,128]{2,0,1:T(8,128)(2,1)S(1)} %get-tuple-element.9), channel_id=1, source_target_pairs={{0,1},{1,2},{2,3},{3,4},{4,5},{5,6},{6,7},{7,8},{8,9},{9,10},{10,1... | collective-permute-start | bytes 98312 | tf_op jit(solution)/shard_map/ppermute | solution.py:13
  52.5 4.5 %collective-permute-start.1 = (bf16[32,4,128]{2,0,1:T(8,128)(2,1)S(1)}, bf16[32,4,128]{2,0,1:T(8,128)(2,1)S(1)}, u32[]{:S(2)}, u32[]{:S(2)}) collective-permute-start(bf16[32,4,128]{2,0,1:T(8,128)(2,1)S(1)} %get-tuple-element.10), channel_id=1, source_target_pairs={{0,127},{1,0},{2,1},{3,2},{4,3},{5,4},{6,5},{7,6},{8,7},{9,8},{10,... | collective-permute-start | bytes 98312 | tf_op jit(solution)/shard_map/ppermute | solution.py:13
  99.7 4.8 %copy-start.2 = (f32[768]{0:T(1024)S(1)}, f32[768]{0:T(1024)}, u32[]{:S(2)}) copy-start(f32[768]{0:T(1024)} %param.15) | copy-start | bytes 9220
  281.9 10.0 %copy-start.1 = (bf16[896,1536]{1,0:T(8,128)(2,1)S(1)}, bf16[896,1536]{1,0:T(8,128)(2,1)}, u32[]{:S(2)}) copy-start(bf16[896,1536]{1,0:T(8,128)(2,1)} %param.11) | copy-start | bytes 8257540
where the time goes:
time: 297 us; the launch traced here: 292 us
  blocking collectives  118 us (40%)
  local copies, waits for them, and re-layouts  77.7 us (26%)
  matrix products  62.9 us (21%)
  starting transfers between devices  18.2 us (6%)
  other arithmetic  7.88 us (3%)
  waiting for transfers between devices  7.46 us (3%)
    all_to_all x1, blocking collectives, on_device(): home = lax.all_to_all(back, 'voc', split_axis=0, concat_axis=0, tiled=True)  118 us
    unnamed x18, local copies, waits for them, and re-layouts  34.1 us
    dot_general x1, local copies, waits for them, and re-layouts, upsample(): jnp.dot(activations.reshape(-1, activations.shape[2]), w_up, preferred_el...  24.6 us
    dot_general x1, matrix products, upsample(): jnp.dot(activations.reshape(-1, activations.shape[2]), w_up, preferred_el...  22.1 us
    dot_general x4, matrix products, move_rows(): jnp.dot(selection.astype(jnp.bfloat16), values.reshape(values.shape[0], -...  20.1 us
    dot_general x1, matrix products, convolve(): result = jnp.dot(flattened, weight, preferred_element_type=jnp.float32)  19.7 us
    all_to_all x1, starting transfers between devices, on_device(): lax.all_to_all(send_info, 'voc', split_axis=0, concat_axis=0, tiled=True)  7.76 us
    all_to_all x1, starting transfers between devices, on_device(): lax.all_to_all(send_feat, 'voc', split_axis=0, concat_axis=0, tiled=True)  6.8 us
  transfers between devices with their start and end apart: 4, of which 3 were waited for; matrix products, arithmetic and copies ran while one was open for 10% of the time, Pallas kernels for 0%

commit v1 on v0

v1 whole, which is shorter than its diff:
```python
import functools

import jax
import jax.numpy as jnp
from jax import lax
from jax.experimental import pallas as pl
from jax.experimental.pallas import tpu as pltpu
from jax.sharding import PartitionSpec as P

UP = 4
KPRE = 7
RIM = 4
CAP = 4
LANES = 128

SIN2 = (9.869604311707747, -32.46967117172015, 42.72719633651888, -30.101465841328583, 13.050098920339147, -3.3565926218240247)


def copy_of(src, dst, sem):
    return pltpu.make_async_copy(src, dst, sem)


def vocode_kernel(starts, frames, block, rims, target, extents, features, *rest):
    if rims:
        home, w_pre, biases, snake, w_up, up_bias, _, out = rest[:8]
        scratch = rest[8:]
    else:
        home = None
        w_pre, biases, snake, w_up, up_bias, out = rest[:6]
        scratch = rest[6:]
    (wp, wu, win, msk, taps, acts, rows32, stage, zeros, slots, ranks, counts, w_sem, out_sem, zero_sem) = scratch
    pieces = len(starts)
    act_rows = frames + 2
    win_rows = frames + 8
    seg = features.shape[1]
    channels = wp.shape[1]
    width = up_bias.shape[1]
    n_slots = target.shape[0]
    span = UP * frames

    copy_of(w_pre, wp, w_sem.at[8]).start()
    order = (2, 6, 3, 7, 4, 0, 5, 1)
    for tap in order:
        cols = pl.ds(tap * width, width)
        copy_of(w_up.at[:, cols], wu.at[:, cols], w_sem.at[tap]).start()

    if not rims:
        zeros[...] = jnp.zeros_like(zeros)
    for v in range(16):
        counts[v] = 0
    slots[0] = 0
    ranks[0] = 0

    def scan(i, found):
        code = target[i]
        used = code >= 0

        @pl.when(used)
        def _():
            worker = code // 32
            rank = counts[worker]
            slots[found] = i
            ranks[found] = rank
            counts[worker] = rank + 1

        if not rims:

            @pl.when(jnp.logical_not(used))
            def _():
                copy_of(zeros, out.at[i], zero_sem.at[i]).start()

        return found + used.astype(jnp.int32)

    found = lax.fori_loop(0, n_slots, scan, jnp.int32(0))
    n_blocks = (found + block - 1) // block

    cell = lax.broadcasted_iota(jnp.int32, (seg, LANES), 0)
    rim_cell = lax.broadcasted_iota(jnp.int32, (2 * RIM, LANES), 0)

    def fill(first, b):
        c = jnp.minimum(first + b, found - 1)
        slot = slots[c]
        own = (cell < extents[slot, 0]).astype(jnp.float32)
        values = features[slot].astype(jnp.float32) * own
        if not rims:
            win[0, pl.ds(b, seg, stride=block), :] = values
            msk[0, pl.ds(b, seg, stride=block), :] = own
        else:
            at = RIM * block + b
            inner = win_rows - RIM
            win[0, pl.ds(at, inner, stride=block), :] = values[:inner]
            msk[0, pl.ds(at, inner, stride=block), :] = own[:inner]
            win[1, pl.ds(b, inner, stride=block), :] = values[seg - inner :]
            msk[1, pl.ds(b, inner, stride=block), :] = own[seg - inner :]
            worker = target[slot] // 32
            rank = ranks[c]
            before_ok = (rim_cell - RIM + seg - RIM < extents[slot, 1]).astype(jnp.float32)
            after_ok = (rim_cell < extents[slot, 2]).astype(jnp.float32)
            before = home[worker, rank].astype(jnp.float32) * before_ok
            after = home[lax.rem(worker + 1, 16), rank].astype(jnp.float32) * after_ok
            win[0, pl.ds(b, RIM, stride=block), :] = before[RIM:]
            msk[0, pl.ds(b, RIM, stride=block), :] = before_ok[RIM:]
            tail = inner * block + b
            win[1, pl.ds(tail, RIM, stride=block), :] = after[:RIM]
            msk[1, pl.ds(tail, RIM, stride=block), :] = after_ok[:RIM]

    def drain(blk):
        buf = lax.rem(blk, 2)

        def one(b, carry):
            @pl.when(blk * block + b < found)
            def _():
                for p in range(pieces):
                    copy_of(stage.at[buf, p, b], out.at[0, pl.ds(0, span)], out_sem.at[buf, p, b]).wait()

            return carry

        lax.fori_loop(0, block, one, 0)

    def body(blk, carry):
        first = blk * block
        buf = lax.rem(blk, 2)

        def fill_one(b, c):
            fill(first, b)
            return c

        lax.fori_loop(0, block, fill_one, 0)

        for p in range(pieces):
            for q in range(KPRE):
                taps[pl.ds(p * act_rows * block, act_rows * block), pl.ds(q * LANES, LANES)] = win[
                    p, pl.ds(q * block, act_rows * block), :
                ].astype(jnp.bfloat16)

        @pl.when(blk == 0)
        def _():
            copy_of(w_pre, wp, w_sem.at[8]).wait()

        step = 256

        def conv_chunk(n, c):
            cols = pl.ds(pl.multiple_of(n * step, step), step)
            bias = biases[:, cols]
            scale = snake[0:1, cols] * (1.0 / jnp.pi)
            inverse = 1.0 / snake[1:2, cols]
            for p in range(pieces):
                sums = jnp.dot(
                    taps[pl.ds(p * act_rows * block, act_rows * block), :],
                    wp[:, cols],
                    preferred_element_type=jnp.float32,
                )
                mask = msk[p, pl.ds(3 * block, act_rows * block), :]
                hidden = jnp.concatenate([mask, mask], axis=1) * (sums + bias)
                turns = hidden * scale
                rest_of = turns - jnp.floor(turns + 0.5)
                u = rest_of * rest_of
                poly = SIN2[-1] * u + SIN2[-2]
                for coef in SIN2[-3::-1]:
                    poly = poly * u + coef
                acts[p, :, cols] = (hidden + u * poly * inverse).astype(jnp.bfloat16)
            return c

        lax.fori_loop(0, channels // step, conv_chunk, 0)

        @pl.when(blk >= 2)
        def _():
            drain(blk - 2)

        for r in range(UP):
            centre_tap = r + UP // 2
            side_tap = r + UP + UP // 2 if r < UP // 2 else r - UP // 2
            side_at = 0 if r < UP // 2 else 2 * block

            @pl.when(blk == 0)
            def _():
                for tap in (centre_tap, side_tap):
                    cols = pl.ds(tap * width, width)
                    copy_of(w_up.at[:, cols], wu.at[:, cols], w_sem.at[tap]).wait()

            def up_chunk(n, c):
                at = pl.multiple_of(n * step, step)
                centre = acts[:, pl.ds(block, frames * block), :].reshape(-1, channels)
                side = acts[:, pl.ds(side_at, frames * block), :].reshape(-1, channels)
                sums = jnp.dot(
                    centre, wu[:, pl.ds(centre_tap * width + at, step)], preferred_element_type=jnp.float32
                ) + jnp.dot(side, wu[:, pl.ds(side_tap * width + at, step)], preferred_element_type=jnp.float32)
                sums = sums + up_bias[:, pl.ds(at, step)]
                for p in range(pieces):
                    for j in range(frames):
                        mask = msk[p, pl.ds((j + 4) * block, block), :]
                        here = (p * frames + j) * block
                        for half in range(step // LANES):
                            rows32[
                                n * (step // LANES) + half,
                                pl.ds(p * block * span + UP * j + r, block, stride=span),
                                :,
                            ] = mask * sums[here : here + block, half * LANES : (half + 1) * LANES]
                return c

            lax.fori_loop(0, width // step, up_chunk, 0)

        def send(b, c):
            for p in range(pieces):
                for n in range(width // LANES):
                    stage[buf, p, b, :, n * LANES : (n + 1) * LANES] = rows32[
                        n, pl.ds((p * block + b) * span, span), :
                    ].astype(jnp.bfloat16)

            @pl.when(first + b < found)
            def _():
                slot = slots[first + b]
                for p in range(pieces):
                    copy_of(
                        stage.at[buf, p, b], out.at[slot, pl.ds(UP * starts[p], span)], out_sem.at[buf, p, b]
                    ).start()

            return c

        lax.fori_loop(0, block, send, 0)
        return carry

    lax.fori_loop(0, n_blocks, body, 0)

    @pl.when(n_blocks == 0)
    def _():
        copy_of(w_pre, wp, w_sem.at[8]).wait()
        for tap in range(2 * UP):
            cols = pl.ds(tap * width, width)
            copy_of(w_up.at[:, cols], wu.at[:, cols], w_sem.at[tap]).wait()

    @pl.when(n_blocks >= 2)
    def _():
        drain(n_blocks - 2)

    @pl.when(n_blocks >= 1)
    def _():
        drain(n_blocks - 1)

    if not rims:

        def settle(i, c):
            @pl.when(target[i] < 0)
            def _():
                copy_of(zeros, out.at[i], zero_sem.at[i]).wait()

            return c

        lax.fori_loop(0, n_slots, settle, 0)


def vocode(starts, frames, block, home, waves, target, extents, features, w_pre, biases, snake, w_up, up_bias):
    rims = home is not None
    pieces = len(starts)
    n_slots, seg, feat = features.shape
    channels = w_pre.shape[1]
    width = up_bias.shape[1]
    span = UP * frames
    smem = pl.BlockSpec(memory_space=pltpu.SMEM)
    vmem = pl.BlockSpec(memory_space=pltpu.VMEM)
    hbm = pl.BlockSpec(memory_space=pl.ANY)
    operands = [target, extents, features]
    specs = [smem, smem, vmem]
    if rims:
        operands.append(home)
        specs.append(vmem)
    operands += [w_pre, biases, snake, w_up, up_bias]
    specs += [hbm, vmem, vmem, hbm, vmem]
    aliases = {}
    if rims:
        aliases = {len(operands): 0}
        operands.append(waves)
        specs.append(hbm)
    return pl.pallas_call(
        functools.partial(vocode_kernel, starts, frames, block, rims),
        out_shape=jax.ShapeDtypeStruct((n_slots, UP * seg, width), jnp.bfloat16),
        in_specs=specs,
        out_specs=hbm,
        input_output_aliases=aliases,
        scratch_shapes=[
            pltpu.VMEM(w_pre.shape, jnp.bfloat16),
            pltpu.VMEM(w_up.shape, jnp.bfloat16),
            pltpu.VMEM((pieces, (frames + 8) * block, feat), jnp.float32),
            pltpu.VMEM((pieces, (frames + 8) * block, feat), jnp.float32),
            pltpu.VMEM((pieces * (frames + 2) * block, KPRE * feat), jnp.bfloat16),
            pltpu.VMEM((pieces, (frames + 2) * block, channels), jnp.bfloat16),
            pltpu.VMEM((width // LANES, pieces * block * span, LANES), jnp.float32),
            pltpu.VMEM((2, pieces, block, span, width), jnp.bfloat16),
            pltpu.VMEM((16, LANES) if rims else (UP * seg, width), jnp.bfloat16),
            pltpu.SMEM((n_slots,), jnp.int32),
            pltpu.SMEM((n_slots,), jnp.int32),
            pltpu.SMEM((16,), jnp.int32),
            pltpu.SemaphoreType.DMA((9,)),
            pltpu.SemaphoreType.DMA((2, pieces, block)),
            pltpu.SemaphoreType.DMA((n_slots,)),
        ],
        compiler_params=pltpu.CompilerParams(vmem_limit_bytes=58 * 2**20),
        cost_estimate=pl.CostEstimate(
            flops=2 * 48 * pieces * frames * 2 * channels * UP * width,
            bytes_accessed=2 * (w_up.size + w_pre.size + 48 * pieces * span * width),
            transcendentals=0,
        ),
        name="edges" if rims else "inner",
    )(*operands)


def one_hot_rows(match, values):
    rows = jnp.dot(match.astype(jnp.bfloat16), values.reshape(values.shape[0], -1), preferred_element_type=jnp.float32)
    return rows.astype(jnp.bfloat16)


def packed(features, target):
    n_slots, seg, feat = features.shape
    used = target >= 0
    worker = jnp.where(used, target // 32, -1)
    hot = (worker[:, None] == jnp.arange(16, dtype=jnp.int32)[None, :]).astype(jnp.int32)
    rank = jnp.sum((jnp.cumsum(hot, axis=0) - hot) * hot, axis=1)
    row = jnp.where(used, worker * CAP + rank, -1)
    select = row[None, :] == jnp.arange(16 * CAP, dtype=jnp.int32)[:, None]
    code = jnp.sum(jnp.where(select, (target % 32 + 1)[None, :], 0), axis=1).astype(jnp.bfloat16)
    heads = one_hot_rows(select, features[:, :RIM]).reshape(16, CAP, RIM, feat)
    tails = one_hot_rows(select, features[:, seg - RIM :]).reshape(16, CAP, RIM, feat)
    tails = jnp.roll(tails, 1, axis=0)
    code = code.reshape(16, CAP)
    codes = jnp.concatenate([jnp.roll(code, 1, axis=0), code], axis=1)
    codes = jnp.broadcast_to(codes[:, None, :, None], (16, 1, 2 * CAP, feat))
    return jnp.concatenate([jnp.concatenate([tails, heads], axis=2), codes], axis=1)


def swapped(got, lower, upper):
    gen, voc = lax.axis_index("gen"), lax.axis_index("voc")
    last = lax.axis_size("gen") - 1
    wraps = voc == 0
    lower = jnp.where(wraps, lower, got)
    upper = jnp.where(wraps, upper, got)

    def codes(block, first):
        return block[:, CAP, first : first + CAP, 0].astype(jnp.int32).reshape(-1)

    def entries(block, first):
        return block[:, :CAP, first : first + RIM]

    tail_code, head_code = codes(got, 0), codes(got, RIM)
    far_tail, far_head = codes(lower, 0), codes(upper, RIM)
    far_tail = jnp.where(wraps & (gen == 0) & (far_tail > 0), far_tail % 32 + 1, far_tail)
    far_head = jnp.where(wraps & (gen == last) & (far_head > 0), (far_head + 30) % 32 + 1, far_head)
    next_match = (tail_code[:, None] == far_head[None, :]) & (tail_code[:, None] > 0)
    prev_match = (head_code[:, None] == far_tail[None, :]) & (head_code[:, None] > 0)
    shape = (got.shape[0], CAP, RIM, got.shape[3])
    heads = one_hot_rows(next_match, entries(upper, RIM).reshape(64, -1)).reshape(shape)
    tails = one_hot_rows(prev_match, entries(lower, 0).reshape(64, -1)).reshape(shape)
    return jnp.concatenate([heads, tails], axis=2)


def on_device(features, target, extents, w_pre, biases, snake_params, w_up, up_bias):
    n_gen, n_voc = lax.axis_size("gen"), lax.axis_size("voc")
    got = lax.all_to_all(packed(features, target), "voc", split_axis=0, concat_axis=0, tiled=True)
    lower = lax.ppermute(got, ("gen", "voc"), [(g * n_voc, (g + 1) % n_gen * n_voc) for g in range(n_gen)])
    upper = lax.ppermute(got, ("gen", "voc"), [(g * n_voc, (g - 1) % n_gen * n_voc) for g in range(n_gen)])
    home = lax.all_to_all(swapped(got, lower, upper), "voc", split_axis=0, concat_axis=0, tiled=True)
    rest = (target, extents, features, w_pre, biases[None, :], snake_params, w_up, up_bias[None, :])
    waves = vocode((RIM,), 16, 16, None, None, *rest)
    return vocode((0, 20), 4, 32, home, waves, *rest)


def solution(mesh):
    split = P(("gen", "voc"))
    return jax.shard_map(
        on_device,
        mesh=mesh,
        in_specs=(split, split, split, P(), P(), P(), P(), P()),
        out_specs=split,
        check_vma=False,
    )
```

time: 297 us -> 114 us (0.38); the launches traced: 292 us -> 113 us
  blocking collectives: 118 us -> 0 us
  Pallas kernels: 0 us -> 75.5 us
  local copies, waits for them, and re-layouts: 77.7 us -> 6.46 us
  matrix products: 62.9 us -> 0.72 us
  starting transfers between devices: 18.2 us -> 24.1 us
  waiting for transfers between devices: 7.46 us -> 1.77 us
  other arithmetic: 7.88 us -> 4.64 us
    all_to_all x1 -> x0, blocking collectives: 118 us -> none  [on_device(): home = lax.all_to_all(back, 'voc', split_axis=0, concat_axis=0, tiled=True)]
    pallas_call x0 -> x2, Pallas kernels: none -> 75.5 us  [vocode(): pl.pallas_call(functools.partial(vocode_kernel, starts, frames, block, ri...]
    dot_general x8 -> x4, matrix products: 62.9 us -> 0.72 us  [one_hot_rows(): jnp.dot(match.astype(jnp.bfloat16), values.reshape(values.shape[0], -1),...]
    unnamed x18 -> x3, local copies, waits for them, and re-layouts: 34.1 us -> 2 us
    dot_general x1 -> x0, local copies, waits for them, and re-layouts: 24.6 us -> none  [upsample(): jnp.dot(activations.reshape(-1, activations.shape[2]), w_up, preferred_el...]
    all_to_all x2, starting transfers between devices: 14.6 us -> 22.7 us  [the longest x1 15 us: on_device(): lax.all_to_all(swapped(got, lower, upper), 'voc', split_axis=0, concat_ax...]
    another operation x1 -> x0, local copies, waits for them, and re-layouts: 6.64 us -> none  [move_rows(): values.reshape(values.shape[0], -1)]
    convert_element_type x1 -> x5, local copies, waits for them, and re-layouts: 5.83 us -> 0.44 us  [the longest x4 0.35 us: codes(): return block[:, CAP, first:first + CAP, 0].astype(jnp.int32).reshape(-1)]
  transfers between devices with their start and end apart: 4 -> 4, of which waited for: 3 -> 1; matrix products, arithmetic and copies ran while one was open for 10% -> 3% of each run, Pallas kernels for 0% -> 39%
where the time goes in v1:
time: 114 us; the launch traced here: 113 us
  Pallas kernels  75.5 us (66%)
  starting transfers between devices  24.1 us (21%)
  local copies, waits for them, and re-layouts  6.46 us (6%)
  other arithmetic  4.64 us (4%)
  waiting for transfers between devices  1.77 us (2%)
    pallas_call x2, Pallas kernels, vocode(): pl.pallas_call(functools.partial(vocode_kernel, starts, frames, block, ri...  75.5 us
    all_to_all x1, starting transfers between devices, on_device(): lax.all_to_all(swapped(got, lower, upper), 'voc', split_axis=0, concat_ax...  15 us
    all_to_all x1, starting transfers between devices, on_device(): lax.all_to_all(packed(features, target), 'voc', split_axis=0, concat_axis...  7.76 us
  transfers between devices with their start and end apart: 4, of which 1 were waited for; matrix products, arithmetic and copies ran while one was open for 3% of the time, Pallas kernels for 39%

profile of v1, /device:TPU:11, one launch (start us, length us, event | category | flops | bytes accessed | tf_op | source)
XLA Modules:
  0.0 113.4 jit_solution(2111826499224189750)
XLA Ops:
  0.0 0.7 compare_select_fusion.8
  0.7 0.1 fusion.8
  0.7 0.1 reduce_window_sum.11
  0.8 0.2 select_reduce_fusion.1
  1.0 0.7 compare_select_fusion.7
  1.7 0.1 select_reduce_fusion
  1.8 0.1 slice_bitcast_fusion
  1.9 0.1 convert_element_type.81
  2.0 0.1 slice.63
  2.1 1.0 fusion.26
  3.1 0.1 convolution_convert_fusion.3
  3.3 0.2 convolution_convert_fusion.2
  3.5 0.1 pad_maximum_fusion.2
  3.6 0.1 broadcast_in_dim.36
  3.7 0.7 pad_maximum_fusion
  4.4 7.8 %all-to-all-start = ((bf16[16,5,8,128]{3,2,1,0:T(8,128)(2,1)}), bf16[16,5,8,128]{3,2,1,0:T(8,128)(2,1)S(1)}, u32[]{:S(2)}, u32[]{:S(2)}) async-start(bf16[16,5,8,128]{3,2,1,0:T(8,128)(2,1)} %pad_maximum_fusion), calls=%async_computation | async-start | bytes 327680 | tf_op jit(solution)/shard_map/all_to_all | solution.py:357
  12.2 1.3 %broadcast_in_dim.38.rest_4_.rest_5_ = f32[1,768]{1,0:T(1,128)} reshape(f32[768]{0:T(1024)} %param.15) | data formatting | bytes 6144 | tf_op jit(solution)/shard_map/broadcast_in_dim | solution.py:361
  13.5 1.3 %broadcast_in_dim.37.rest_1_.rest_2_ = f32[1,1536]{1,0:T(1,128)} reshape(f32[1536]{0:T(1024)} %param.12) | data formatting | bytes 12288 | tf_op jit(solution)/shard_map/broadcast_in_dim | solution.py:361
  14.8 1.4 %copy.23.extents = s32[64,3]{1,0:T(8,128)} copy(s32[64,3]{0,1:T(4,128)} %param.10) | data formatting | bytes 1536 | tf_op args[2]
  16.1 1.8 %all-to-all-done = bf16[16,5,8,128]{3,2,1,0:T(8,128)(2,1)S(1)} async-done(((bf16[16,5,8,128]{3,2,1,0:T(8,128)(2,1)}), bf16[16,5,8,128]{3,2,1,0:T(8,128)(2,1)S(1)}, u32[]{:S(2)}, u32[]{:S(2)}) %all-to-all-start) | async-done | bytes 163872 | tf_op jit(solution)/shard_map/all_to_all | solution.py:357
  17.9 0.6 convert_reduce_fusion.3
  18.5 0.1 reshape.122
  18.6 0.1 reshape.124
  18.7 0.7 collective-permute-start.1
  19.4 0.7 collective-permute-start
  20.1 0.0 collective-permute-done.1
  20.1 0.0 collective-permute-done
  20.2 0.6 convert_reduce_fusion
  20.8 0.1 reshape.125
  20.9 0.2 convolution_convert_fusion
  21.2 0.1 reshape.123
  21.3 0.2 convolution_convert_fusion.1
  21.5 0.7 pad_maximum_fusion.1
  22.2 15.0 %all-to-all-start.1 = ((bf16[16,4,8,128]{3,2,1,0:T(8,128)(2,1)}), bf16[16,4,8,128]{3,2,1,0:T(8,128)(2,1)S(1)}, u32[]{:S(2)}, u32[]{:S(2)}) async-start(bf16[16,4,8,128]{3,2,1,0:T(8,128)(2,1)} %pad_maximum_fusion.1), calls=%async_computation.1 | async-start | bytes 262144 | tf_op jit(solution)/shard_map/all_to_all | solution.py:360
  37.2 44.2 %inner.1.rest_6_ = bf16[64,96,768]{2,1,0:T(8,128)(2,1)} custom-call(s32[64]{0:T(128)} %target.3, s32[64,3]{1,0:T(8,128)} %copy.23.extents, bf16[64,24,128]{2,1,0:T(8,128)(2,1)} %features.3, bf16[896,1536]{1,0:T(8,128)(2,1)} %rest_1_.1, f32[1,1536]{1,0:T(1,128)} %broadcast_in_dim.37.rest_1_.rest_2_, f32[2,1536]{1,0:T(2,128)} %rest_3_.3, ...), custom_call_target="tpu_custom_call" | custom-call | flops 14495514624 | bytes 26345472 | tf_op jit(solution)/shard_map/inner/pallas_call | solution.py:274
  81.5 0.0 all-to-all-done.1.rest_0_
  81.5 0.0 copy-start
  81.5 0.6 copy-done
  82.1 31.3 %edges.1 = bf16[64,96,768]{2,1,0:T(8,128)(2,1)} custom-call(s32[64]{0:T(128)} %target.3, s32[64,3]{1,0:T(8,128)} %copy.23.extents, bf16[64,24,128]{2,1,0:T(8,128)(2,1)} %features.3, bf16[16,4,8,128]{3,2,1,0:T(8,128)(2,1)} %copy-done, bf16[896,1536]{1,0:T(8,128)(2,1)} %rest_1_.1, ...), custom_call_target="tpu_custom_call", output_to_operand_aliasing={{}: (9, {})} | custom-call | flops 7247757312 | bytes 23986176 | tf_op jit(solution)/shard_map/edges/pallas_call | solution.py:274
  (14 shorter events, 0.3 us)
Async XLA Ops:
  4.4 13.5 %all-to-all-start = ((bf16[16,5,8,128]{3,2,1,0:T(8,128)(2,1)}), bf16[16,5,8,128]{3,2,1,0:T(8,128)(2,1)S(1)}, u32[]{:S(2)}, u32[]{:S(2)}) async-start(bf16[16,5,8,128]{3,2,1,0:T(8,128)(2,1)} %pad_maximum_fusion), calls=%async_computation | async-start | bytes 327680 | tf_op jit(solution)/shard_map/all_to_all | solution.py:357
  18.7 1.4 %collective-permute-start.1 = (bf16[16,5,8,128]{3,2,1,0:T(8,128)(2,1)S(1)}, bf16[16,5,8,128]{3,2,1,0:T(8,128)(2,1)S(1)}, u32[]{:S(2)}, u32[]{:S(2)}) collective-permute-start(bf16[16,5,8,128]{3,2,1,0:T(8,128)(2,1)S(1)} %all-to-all-done), channel_id=1, source_target_pairs={{0,16},{16,32},{32,48},{48,64},{64,80},{80,96},{96,112},{112,0}} | collective-permute-start | bytes 491528 | tf_op jit(solution)/shard_map/ppermute | solution.py:358
  19.4 0.7 collective-permute-start
  22.2 59.2 %all-to-all-start.1 = ((bf16[16,4,8,128]{3,2,1,0:T(8,128)(2,1)}), bf16[16,4,8,128]{3,2,1,0:T(8,128)(2,1)S(1)}, u32[]{:S(2)}, u32[]{:S(2)}) async-start(bf16[16,4,8,128]{3,2,1,0:T(8,128)(2,1)} %pad_maximum_fusion.1), calls=%async_computation.1 | async-start | bytes 262144 | tf_op jit(solution)/shard_map/all_to_all | solution.py:360
  81.5 0.6 copy-start

commit v2 on v1

v2 whole, which is shorter than its diff:
```python
import functools

import jax
import jax.numpy as jnp
from jax import lax
from jax.experimental import pallas as pl
from jax.experimental.pallas import tpu as pltpu
from jax.sharding import PartitionSpec as P

UP = 4
KPRE = 7
RIM = 4
CAP = 4
LANES = 128
STEP = 256

SIN2 = (9.869604311707747, -32.46967117172015, 42.72719633651888, -30.101465841328583, 13.050098920339147, -3.3565926218240247)


def copy_of(src, dst, sem):
    return pltpu.make_async_copy(src, dst, sem)


def vocode_kernel(starts, frames, rims, target, extents, features, *rest):
    if rims:
        home, w_pre, biases, snake, w_up, up_bias, _, out = rest[:8]
        scratch = rest[8:]
    else:
        home = None
        w_pre, biases, snake, w_up, up_bias, out = rest[:6]
        scratch = rest[6:]
    (wp, wu, win, msk, taps, acts, rows32, stage, zeros, slots, ranks, counts, w_sem, out_sem, zero_sem) = scratch
    pieces = len(starts)
    act_rows = frames + 2
    win_rows = frames + 8
    seg = features.shape[1]
    channels = wp.shape[1]
    width = up_bias.shape[1]
    n_slots = target.shape[0]
    span = UP * frames
    pitch = span + 8
    parts = width // STEP
    tiles = STEP // LANES

    phases = tuple((r + UP // 2, r + UP + UP // 2 if r < UP // 2 else r - UP // 2) for r in range(UP))

    def load_taps(n, start):
        for tap in sum(phases, ()):
            cols = pl.ds(pl.multiple_of(tap * width + n * STEP, STEP), STEP)
            copy = copy_of(w_up.at[:, cols], wu.at[:, cols], w_sem.at[n, tap])
            copy.start() if start else copy.wait()

    def load_pre(start):
        copy = copy_of(w_pre, wp, w_sem.at[parts, 0])
        copy.start() if start else copy.wait()

    load_pre(True)
    for v in range(17):
        counts[v] = 0
    slots[0] = 0
    ranks[0] = 0

    def scan(i, found):
        code = target[i]
        used = code >= 0
        slots[found] = i
        if rims:
            worker = jnp.where(used, lax.shift_right_logical(code, 5), 16)
            rank = counts[worker]
            ranks[found] = rank
            counts[worker] = rank + 1
        return found + used.astype(jnp.int32)

    found = lax.fori_loop(0, n_slots, scan, jnp.int32(0), unroll=8)

    cell = lax.broadcasted_iota(jnp.int32, (seg, LANES), 0)
    rim_cell = lax.broadcasted_iota(jnp.int32, (2 * RIM, LANES), 0)

    def fill(block, b):
        c = jnp.minimum(b, found - 1)
        slot = slots[c]
        own = (cell < extents[slot, 0]).astype(jnp.float32)
        values = features[slot].astype(jnp.float32) * own
        if not rims:
            win[0, pl.ds(b, seg, stride=block), :] = values
            msk[0, pl.ds(b, seg, stride=block), :] = own
        else:
            at = RIM * block + b
            inner = win_rows - RIM
            win[0, pl.ds(at, inner, stride=block), :] = values[:inner]
            msk[0, pl.ds(at, inner, stride=block), :] = own[:inner]
            win[1, pl.ds(b, inner, stride=block), :] = values[seg - inner :]
            msk[1, pl.ds(b, inner, stride=block), :] = own[seg - inner :]
            worker = lax.shift_right_logical(target[slot], 5)
            rank = ranks[c]
            before_ok = (rim_cell - RIM + seg - RIM < extents[slot, 1]).astype(jnp.float32)
            after_ok = (rim_cell < extents[slot, 2]).astype(jnp.float32)
            before = home[worker, rank].astype(jnp.float32) * before_ok
            after = home[(worker + 1) & 15, rank].astype(jnp.float32) * after_ok
            win[0, pl.ds(b, RIM, stride=block), :] = before[RIM:]
            msk[0, pl.ds(b, RIM, stride=block), :] = before_ok[RIM:]
            tail = inner * block + b
            win[1, pl.ds(tail, RIM, stride=block), :] = after[:RIM]
            msk[1, pl.ds(tail, RIM, stride=block), :] = after_ok[:RIM]

    def run(block):
        rows = act_rows * block

        def fill_one(b, c):
            fill(block, b)
            return c

        lax.fori_loop(0, block, fill_one, 0, unroll=2)
        for p in range(pieces):
            for q in range(KPRE):
                taps[pl.ds(p * rows, rows), pl.ds(q * LANES, LANES)] = win[p, pl.ds(q * block, rows), :].astype(
                    jnp.bfloat16
                )

        load_pre(False)
        for n in range(parts):
            load_taps(n, True)

        if not rims:
            zeros[...] = jnp.zeros_like(zeros)

            def clear(i, c):
                @pl.when(target[i] < 0)
                def _():
                    copy_of(zeros, out.at[i], zero_sem.at[i]).start()

                return c

            lax.fori_loop(0, n_slots, clear, 0)

        def conv_chunk(n, c):
            cols = pl.ds(pl.multiple_of(n * STEP, STEP), STEP)
            bias = biases[:, cols]
            scale = snake[0:1, cols] * (1.0 / jnp.pi)
            inverse = 1.0 / snake[1:2, cols]
            for p in range(pieces):
                sums = jnp.dot(taps[pl.ds(p * rows, rows), :], wp[:, cols], preferred_element_type=jnp.float32)
                mask = msk[p, pl.ds(3 * block, rows), :]
                hidden = jnp.concatenate([mask] * tiles, axis=1) * (sums + bias)
                turns = hidden * scale
                rest_of = turns - jnp.floor(turns + 0.5)
                u = rest_of * rest_of
                poly = SIN2[-1] * u + SIN2[-2]
                for coef in SIN2[-3::-1]:
                    poly = poly * u + coef
                acts[pl.ds(p * rows, rows), cols] = (hidden + u * poly * inverse).astype(jnp.bfloat16)
            return c

        lax.fori_loop(0, channels // STEP, conv_chunk, 0, unroll=2)

        def acts_from(shift):
            picked = [acts[pl.ds(p * rows + shift * block, frames * block), :] for p in range(pieces)]
            return picked[0] if pieces == 1 else jnp.concatenate(picked, axis=0)

        def up_part(n, c):
            load_taps(n, False)
            for r in range(UP):
                sums = up_bias[:, pl.ds(pl.multiple_of(n * STEP, STEP), STEP)]
                for tap, shift in zip(phases[r], (1, 0 if r < UP // 2 else 2)):
                    cols = pl.ds(pl.multiple_of(tap * width + n * STEP, STEP), STEP)
                    sums = sums + jnp.dot(acts_from(shift), wu[:, cols], preferred_element_type=jnp.float32)
                for p in range(pieces):
                    for j in range(frames):
                        mask = msk[p, pl.ds((j + 4) * block, block), :]
                        here = (p * frames + j) * block
                        for half in range(tiles):
                            rows32[
                                n * tiles + half, pl.ds(p * block * pitch + UP * j + r, block, stride=pitch), :
                            ] = mask * sums[here : here + block, half * LANES : (half + 1) * LANES]
            return c

        lax.fori_loop(0, parts, up_part, 0)

        def send(b, c):
            for p in range(pieces):
                for n in range(width // LANES):
                    stage[p, b, :, n * LANES : (n + 1) * LANES] = rows32[
                        n, pl.ds(pl.multiple_of((p * block + b) * pitch, 8), span), :
                    ].astype(jnp.bfloat16)

            @pl.when(b < found)
            def _():
                for p in range(pieces):
                    copy_of(stage.at[p, b], out.at[slots[b], pl.ds(UP * starts[p], span)], out_sem.at[p, b]).start()

            return c

        lax.fori_loop(0, block, send, 0)

    for units in range(1, 5):

        @pl.when((found > 16 * (units - 1)) & (found <= 16 * units))
        def _(units=units):
            run(16 * units)

    @pl.when(found == 0)
    def _():
        load_pre(False)
        if not rims:
            zeros[...] = jnp.zeros_like(zeros)

            def clear(i, c):
                copy_of(zeros, out.at[i], zero_sem.at[i]).start()
                return c

            lax.fori_loop(0, n_slots, clear, 0)

    def settle(b, c):
        @pl.when(b < found)
        def _():
            for p in range(pieces):
                copy_of(stage.at[p, b], out.at[0, pl.ds(0, span)], out_sem.at[p, b]).wait()

        if not rims:

            @pl.when(target[b] < 0)
            def _():
                copy_of(zeros, out.at[b], zero_sem.at[b]).wait()

        return c

    lax.fori_loop(0, n_slots, settle, 0)


def vocode(starts, frames, home, waves, target, extents, features, w_pre, biases, snake, w_up, up_bias):
    rims = home is not None
    pieces = len(starts)
    n_slots, seg, feat = features.shape
    channels = w_pre.shape[1]
    width = up_bias.shape[1]
    span = UP * frames
    pitch = span + 8
    smem = pl.BlockSpec(memory_space=pltpu.SMEM)
    vmem = pl.BlockSpec(memory_space=pltpu.VMEM)
    hbm = pl.BlockSpec(memory_space=pl.ANY)
    operands = [target, extents, features]
    specs = [smem, smem, vmem]
    if rims:
        operands.append(home)
        specs.append(vmem)
    operands += [w_pre, biases, snake, w_up, up_bias]
    specs += [hbm, vmem, vmem, hbm, vmem]
    aliases = {}
    if rims:
        aliases = {len(operands): 0}
        operands.append(waves)
        specs.append(hbm)
    return pl.pallas_call(
        functools.partial(vocode_kernel, starts, frames, rims),
        out_shape=jax.ShapeDtypeStruct((n_slots, UP * seg, width), jnp.bfloat16),
        in_specs=specs,
        out_specs=hbm,
        input_output_aliases=aliases,
        scratch_shapes=[
            pltpu.VMEM(w_pre.shape, jnp.bfloat16),
            pltpu.VMEM(w_up.shape, jnp.bfloat16),
            pltpu.VMEM((pieces, (frames + 8) * n_slots, feat), jnp.float32),
            pltpu.VMEM((pieces, (frames + 8) * n_slots, feat), jnp.float32),
            pltpu.VMEM((pieces * (frames + 2) * n_slots, KPRE * feat), jnp.bfloat16),
            pltpu.VMEM((pieces * (frames + 2) * n_slots, channels), jnp.bfloat16),
            pltpu.VMEM((width // LANES, pieces * n_slots * (span + 8), LANES), jnp.float32),
            pltpu.VMEM((pieces, n_slots, span, width), jnp.bfloat16),
            pltpu.VMEM((16, LANES) if rims else (UP * seg, width), jnp.bfloat16),
            pltpu.SMEM((n_slots + 1,), jnp.int32),
            pltpu.SMEM((n_slots + 1,), jnp.int32),
            pltpu.SMEM((17,), jnp.int32),
            pltpu.SemaphoreType.DMA((width // STEP + 1, 2 * UP)),
            pltpu.SemaphoreType.DMA((pieces, n_slots)),
            pltpu.SemaphoreType.DMA((n_slots,)),
        ],
        compiler_params=pltpu.CompilerParams(vmem_limit_bytes=58 * 2**20),
        cost_estimate=pl.CostEstimate(
            flops=2 * 48 * pieces * frames * 2 * channels * UP * width,
            bytes_accessed=2 * (w_up.size + w_pre.size + 48 * pieces * span * width),
            transcendentals=0,
        ),
        name="edges" if rims else "inner",
    )(*operands)


def one_hot_rows(match, values):
    rows = jnp.dot(match.astype(jnp.bfloat16), values.reshape(values.shape[0], -1), preferred_element_type=jnp.float32)
    return rows.astype(jnp.bfloat16)


def packed(features, target):
    n_slots, seg, feat = features.shape
    used = target >= 0
    worker = jnp.where(used, target // 32, -1)
    hot = (worker[:, None] == jnp.arange(16, dtype=jnp.int32)[None, :]).astype(jnp.int32)
    rank = jnp.sum((jnp.cumsum(hot, axis=0) - hot) * hot, axis=1)
    row = jnp.where(used, worker * CAP + rank, -1)
    select = row[None, :] == jnp.arange(16 * CAP, dtype=jnp.int32)[:, None]
    code = jnp.sum(jnp.where(select, (target % 32 + 1)[None, :], 0), axis=1).astype(jnp.bfloat16)
    heads = one_hot_rows(select, features[:, :RIM]).reshape(16, CAP, RIM, feat)
    tails = one_hot_rows(select, features[:, seg - RIM :]).reshape(16, CAP, RIM, feat)
    tails = jnp.roll(tails, 1, axis=0)
    code = code.reshape(16, CAP)
    codes = jnp.concatenate([jnp.roll(code, 1, axis=0), code], axis=1)
    codes = jnp.broadcast_to(codes[:, None, :, None], (16, 1, 2 * CAP, feat))
    return jnp.concatenate([jnp.concatenate([tails, heads], axis=2), codes], axis=1)


def swapped(got, lower, upper):
    gen, voc = lax.axis_index("gen"), lax.axis_index("voc")
    last = lax.axis_size("gen") - 1
    wraps = voc == 0
    lower = jnp.where(wraps, lower, got)
    upper = jnp.where(wraps, upper, got)

    def codes(block, first):
        return block[:, CAP, first : first + CAP, 0].astype(jnp.int32).reshape(-1)

    def entries(block, first):
        return block[:, :CAP, first : first + RIM]

    tail_code, head_code = codes(got, 0), codes(got, RIM)
    far_tail, far_head = codes(lower, 0), codes(upper, RIM)
    far_tail = jnp.where(wraps & (gen == 0) & (far_tail > 0), far_tail % 32 + 1, far_tail)
    far_head = jnp.where(wraps & (gen == last) & (far_head > 0), (far_head + 30) % 32 + 1, far_head)
    next_match = (tail_code[:, None] == far_head[None, :]) & (tail_code[:, None] > 0)
    prev_match = (head_code[:, None] == far_tail[None, :]) & (head_code[:, None] > 0)
    shape = (got.shape[0], CAP, RIM, got.shape[3])
    heads = one_hot_rows(next_match, entries(upper, RIM).reshape(64, -1)).reshape(shape)
    tails = one_hot_rows(prev_match, entries(lower, 0).reshape(64, -1)).reshape(shape)
    return jnp.concatenate([heads, tails], axis=2)


def on_device(features, target, extents, w_pre, biases, snake_params, w_up, up_bias):
    n_gen, n_voc = lax.axis_size("gen"), lax.axis_size("voc")
    got = lax.all_to_all(packed(features, target), "voc", split_axis=0, concat_axis=0, tiled=True)
    lower = lax.ppermute(got, ("gen", "voc"), [(g * n_voc, (g + 1) % n_gen * n_voc) for g in range(n_gen)])
    upper = lax.ppermute(got, ("gen", "voc"), [(g * n_voc, (g - 1) % n_gen * n_voc) for g in range(n_gen)])
    home = lax.all_to_all(swapped(got, lower, upper), "voc", split_axis=0, concat_axis=0, tiled=True)
    rest = (target, extents, features, w_pre, biases[None, :], snake_params, w_up, up_bias[None, :])
    waves = vocode((RIM,), 16, None, None, *rest)
    return vocode((0, 20), 4, home, waves, *rest)


def solution(mesh):
    split = P(("gen", "voc"))
    return jax.shard_map(
        on_device,
        mesh=mesh,
        in_specs=(split, split, split, P(), P(), P(), P(), P()),
        out_specs=split,
        check_vma=False,
    )
```

time: 114 us -> 86.9 us (0.76)
  Pallas kernels: 75.5 us -> 47.7 us
    pallas_call x2, Pallas kernels: 75.5 us -> 47.7 us  [vocode(): pl.pallas_call(functools.partial(vocode_kernel, starts, frames, rims), ou...]
  transfers between devices with their start and end apart: 4 -> 4, of which waited for: 1 -> 1; matrix products, arithmetic and copies ran while one was open for 3% -> 5% of each run, Pallas kernels for 39% -> 34%
where the time goes in v2:
time: 86.9 us; the launch traced here: 85.7 us
  Pallas kernels  47.7 us (55%)
  starting transfers between devices  24.1 us (28%)
  local copies, waits for them, and re-layouts  6.46 us (7%)
  other arithmetic  4.64 us (5%)
  waiting for transfers between devices  1.77 us (2%)
    pallas_call x2, Pallas kernels, vocode(): pl.pallas_call(functools.partial(vocode_kernel, starts, frames, rims), ou...  47.7 us
    all_to_all x1, starting transfers between devices, on_device(): lax.all_to_all(swapped(got, lower, upper), 'voc', split_axis=0, concat_ax...  15 us
    all_to_all x1, starting transfers between devices, on_device(): lax.all_to_all(packed(features, target), 'voc', split_axis=0, concat_axis...  7.76 us
    unnamed x3, local copies, waits for them, and re-layouts  2 us
    all_to_all x1, waiting for transfers between devices, on_device(): lax.all_to_all(packed(features, target), 'voc', split_axis=0, concat_axis...  1.76 us
  transfers between devices with their start and end apart: 4, of which 1 were waited for; matrix products, arithmetic and copies ran while one was open for 5% of the time, Pallas kernels for 34%

profile of v2, /device:TPU:11, one launch (start us, length us, event | category | flops | bytes accessed | tf_op | source)
XLA Modules:
  0.0 85.7 jit_solution(18064131639597852442)
XLA Ops:
  0.0 0.7 compare_select_fusion.8
  0.7 0.1 fusion.8
  0.7 0.1 reduce_window_sum.11
  0.8 0.2 select_reduce_fusion.1
  1.0 0.7 compare_select_fusion.7
  1.7 0.1 select_reduce_fusion
  1.8 0.1 slice_bitcast_fusion
  1.9 0.1 convert_element_type.81
  2.0 0.1 slice.63
  2.1 1.0 %fusion.26 = (bf16[64,4,128]{2,1,0:T(4,128)(2,1)S(1)}, bf16[64,4,128]{2,1,0:T(4,128)(2,1)S(1)}) fusion(bf16[64,24,128]{2,1,0:T(8,128)(2,1)} %features.3), kind=kLoop, calls=%fused_computation.61 | loop fusion | bytes 262144 | tf_op jit(solution)/shard_map/slice | solution.py:301
  3.1 0.1 convolution_convert_fusion.3
  3.3 0.2 convolution_convert_fusion.2
  3.5 0.1 pad_maximum_fusion.2
  3.6 0.1 broadcast_in_dim.36
  3.7 0.7 pad_maximum_fusion
  4.4 7.8 %all-to-all-start = ((bf16[16,5,8,128]{3,2,1,0:T(8,128)(2,1)}), bf16[16,5,8,128]{3,2,1,0:T(8,128)(2,1)S(1)}, u32[]{:S(2)}, u32[]{:S(2)}) async-start(bf16[16,5,8,128]{3,2,1,0:T(8,128)(2,1)} %pad_maximum_fusion), calls=%async_computation | async-start | bytes 327680 | tf_op jit(solution)/shard_map/all_to_all | solution.py:336
  12.2 1.3 %broadcast_in_dim.38.rest_4_.rest_5_ = f32[1,768]{1,0:T(1,128)} reshape(f32[768]{0:T(1024)} %param.15) | data formatting | bytes 6144 | tf_op jit(solution)/shard_map/broadcast_in_dim | solution.py:340
  13.5 1.3 %broadcast_in_dim.37.rest_1_.rest_2_ = f32[1,1536]{1,0:T(1,128)} reshape(f32[1536]{0:T(1024)} %param.12) | data formatting | bytes 12288 | tf_op jit(solution)/shard_map/broadcast_in_dim | solution.py:340
  14.8 1.4 %copy.23.extents = s32[64,3]{1,0:T(8,128)} copy(s32[64,3]{0,1:T(4,128)} %param.10) | data formatting | bytes 1536 | tf_op args[2]
  16.1 1.8 %all-to-all-done = bf16[16,5,8,128]{3,2,1,0:T(8,128)(2,1)S(1)} async-done(((bf16[16,5,8,128]{3,2,1,0:T(8,128)(2,1)}), bf16[16,5,8,128]{3,2,1,0:T(8,128)(2,1)S(1)}, u32[]{:S(2)}, u32[]{:S(2)}) %all-to-all-start) | async-done | bytes 163872 | tf_op jit(solution)/shard_map/all_to_all | solution.py:336
  17.9 0.6 convert_reduce_fusion.3
  18.5 0.1 reshape.122
  18.6 0.1 reshape.124
  18.7 0.7 collective-permute-start.1
  19.4 0.7 collective-permute-start
  20.1 0.0 collective-permute-done.1
  20.1 0.0 collective-permute-done
  20.2 0.6 convert_reduce_fusion
  20.8 0.1 reshape.125
  20.9 0.2 convolution_convert_fusion
  21.2 0.1 reshape.123
  21.3 0.2 convolution_convert_fusion.1
  21.5 0.7 pad_maximum_fusion.1
  22.2 15.0 %all-to-all-start.1 = ((bf16[16,4,8,128]{3,2,1,0:T(8,128)(2,1)}), bf16[16,4,8,128]{3,2,1,0:T(8,128)(2,1)S(1)}, u32[]{:S(2)}, u32[]{:S(2)}) async-start(bf16[16,4,8,128]{3,2,1,0:T(8,128)(2,1)} %pad_maximum_fusion.1), calls=%async_computation.1 | async-start | bytes 262144 | tf_op jit(solution)/shard_map/all_to_all | solution.py:339
  37.2 28.9 %inner.1.rest_6_ = bf16[64,96,768]{2,1,0:T(8,128)(2,1)} custom-call(s32[64]{0:T(128)} %target.3, s32[64,3]{1,0:T(8,128)} %copy.23.extents, bf16[64,24,128]{2,1,0:T(8,128)(2,1)} %features.3, bf16[896,1536]{1,0:T(8,128)(2,1)} %rest_1_.1, f32[1,1536]{1,0:T(1,128)} %broadcast_in_dim.37.rest_1_.rest_2_, f32[2,1536]{1,0:T(2,128)} %rest_3_.3, ...), custom_call_target="tpu_custom_call" | custom-call | flops 14495514624 | bytes 26345472 | tf_op jit(solution)/shard_map/inner/pallas_call | solution.py:253
  66.1 0.0 all-to-all-done.1.rest_0_
  66.1 0.0 copy-start
  66.1 0.6 copy-done
  66.8 18.8 %edges.1 = bf16[64,96,768]{2,1,0:T(8,128)(2,1)} custom-call(s32[64]{0:T(128)} %target.3, s32[64,3]{1,0:T(8,128)} %copy.23.extents, bf16[64,24,128]{2,1,0:T(8,128)(2,1)} %features.3, bf16[16,4,8,128]{3,2,1,0:T(8,128)(2,1)} %copy-done, bf16[896,1536]{1,0:T(8,128)(2,1)} %rest_1_.1, ...), custom_call_target="tpu_custom_call", output_to_operand_aliasing={{}: (9, {})} | custom-call | flops 7247757312 | bytes 23986176 | tf_op jit(solution)/shard_map/edges/pallas_call | solution.py:253
  (14 shorter events, 0.3 us)
Async XLA Ops:
  4.4 13.5 %all-to-all-start = ((bf16[16,5,8,128]{3,2,1,0:T(8,128)(2,1)}), bf16[16,5,8,128]{3,2,1,0:T(8,128)(2,1)S(1)}, u32[]{:S(2)}, u32[]{:S(2)}) async-start(bf16[16,5,8,128]{3,2,1,0:T(8,128)(2,1)} %pad_maximum_fusion), calls=%async_computation | async-start | bytes 327680 | tf_op jit(solution)/shard_map/all_to_all | solution.py:336
  18.7 1.4 %collective-permute-start.1 = (bf16[16,5,8,128]{3,2,1,0:T(8,128)(2,1)S(1)}, bf16[16,5,8,128]{3,2,1,0:T(8,128)(2,1)S(1)}, u32[]{:S(2)}, u32[]{:S(2)}) collective-permute-start(bf16[16,5,8,128]{3,2,1,0:T(8,128)(2,1)S(1)} %all-to-all-done), channel_id=1, source_target_pairs={{0,16},{16,32},{32,48},{48,64},{64,80},{80,96},{96,112},{112,0}} | collective-permute-start | bytes 491528 | tf_op jit(solution)/shard_map/ppermute | solution.py:337
  19.4 0.7 collective-permute-start
  22.2 43.9 %all-to-all-start.1 = ((bf16[16,4,8,128]{3,2,1,0:T(8,128)(2,1)}), bf16[16,4,8,128]{3,2,1,0:T(8,128)(2,1)S(1)}, u32[]{:S(2)}, u32[]{:S(2)}) async-start(bf16[16,4,8,128]{3,2,1,0:T(8,128)(2,1)} %pad_maximum_fusion.1), calls=%async_computation.1 | async-start | bytes 262144 | tf_op jit(solution)/shard_map/all_to_all | solution.py:339
  66.1 0.6 copy-start
